TPU v7x, 128 devices: a whole 4x4x4 slice. The times are simulated.
128 devices in a mesh: cube: 8 (over x_hi, z), front: 16 (over y, x_lo, core).
Axes of the slice: x: 4 (x_hi: 2, x_lo: 2; x = x_hi * 2 + x_lo), y: 4, z: 4, core: 2. Of those that a mesh axis runs over, the one named last changes fastest.
Arguments:
- child_block: float32 [8, 16, 14, 128, 512], P('cube', 'front'), may hold values from -4 to 4, as said below
- child_rows: int32 [8, 16, 14], P('cube', 'front'), may hold values from 0 to 255, as said below
- child_cols: int32 [8, 4], P('cube'), may hold values from 0 to 5, as said below
- parent_base: float32 [8, 16, 8, 128, 768], P('cube', 'front'), may hold values from -16 to 36, as said below
Outputs:
- lower_factor: float32 [8, 16, 8, 128, 768], P('cube', 'front')
Inputs may be any that keep to these rules, and one draw needn't show every extreme that they name: `child_rows`: group g's child feeds the front of pair g // 2. The 14 tiles at front index f go to distinct increasing parent tiles within 2 * 16 * (f % 8) to 2 * 16 * (f % 8 + 1) - 1; each child's first tile goes to 0 and its last to 255. `child_cols`: distinct and increasing for each group; the first is 0 and the last 5. `child_block`: rows of tiles that go to parent tiles under 6 lie within -0.005 to 0.005. `parent_base`: the first 768 rows of each front form a symmetric matrix whose smallest eigenvalue is 10 or more.
All inputs are finite; a program needn't handle non-finite values.
Results may differ from a plain program's by a relative error of at most 0.0001.
Values sent between devices are 32-bit elements; how exact they have to be, the bound alone decides.
A program may use at most 128 MiB of HBM per device.

v0:
```python
import jax
import jax.numpy as jnp
from jax import lax
from jax.experimental import pallas as pl
from jax.experimental.pallas import tpu as pltpu
from jax.sharding import Mesh
from jax.sharding import PartitionSpec as P

MESH = pl.DeviceIdType.MESH
HI = lax.Precision.HIGHEST
VM = pl.BlockSpec(memory_space=pltpu.VMEM)
ANY = pl.BlockSpec(memory_space=pl.ANY)
SM = pl.BlockSpec(memory_space=pltpu.SMEM)


def nt(a,b,prec=HI):
    return lax.dot_general(a,b,(((1,),(1,)),((),())),precision=prec,preferred_element_type=jnp.float32)
def nn(a,b,prec=HI):
    return lax.dot_general(a,b,(((1,),(0,)),((),())),precision=prec,preferred_element_type=jnp.float32)
def full(x): return jnp.broadcast_to(x,(8,128))
def base(block):
    sub=lax.broadcasted_iota(jnp.int32,(8,128),0)
    S=block
    T=jnp.where(lax.broadcasted_iota(jnp.int32,(128,128),0)==lax.broadcasted_iota(jnp.int32,(128,128),1),1.0,0.0).astype(jnp.float32)
    U=[];M=[]
    for s in range(16):
        n=128-8*s
        R=S[:8]; Q=T[:8]
        C=[full(R[:,8*s+j:8*s+j+1]) for j in range(8)]
        D={(i,j):full(C[j][i:i+1]) for i in range(8) for j in range(i,8)}
        ra=[None]*8; E={}
        for p in range(0,8,2):
            a,b,c=D[p,p],D[p,p+1],D[p+1,p+1]
            rs=lax.rsqrt(a*c-b*b); rd=rs*rs
            A,B,Cc=c*rd,b*rd,a*rd
            r0=lax.rsqrt(a); ra[p]=r0; ra[p+1]=(a*r0)*rs; E[p+1,p]=b*(r0*r0)
            for i in range(p+2,8):
                x0,x1=D[p,i],D[p+1,i]
                e0=x0*A-x1*B; e1=x1*Cc-x0*B
                E[i,p]=e0; E[i,p+1]=e1
                for j in range(i,8):
                    D[i,j]=D[i,j]-(e0*D[p,j]+e1*D[p+1,j])
        W=[full(R[i:i+1]) for i in range(8)]; V=[full(Q[i:i+1]) for i in range(8)]
        for p in range(0,8,2):
            for i in range(p+2,8):
                W[i]=W[i]-(E[i,p]*W[p]+E[i,p+1]*W[p+1]); V[i]=V[i]-(E[i,p]*V[p]+E[i,p+1]*V[p+1])
        for p in range(0,8,2):
            W[p+1]=W[p+1]-E[p+1,p]*W[p]; V[p+1]=V[p+1]-E[p+1,p]*V[p]
        W=[w*r for w,r in zip(W,ra)]; V=[v*r for v,r in zip(V,ra)]
        def merge(rows):
            o=rows[7]
            for k in range(7): o=jnp.where(sub==k,rows[k],o)
            return o
        U.append(merge(W)); M.append(merge(V))
        if s<15:
            S=S[8:]; T=T[8:]
            rows=[]; trows=[]
            for t in range((n-8)//8):
                St=S[8*t:8*t+8]; Tt=T[8*t:8*t+8]
                Z=[full(St[:,8*s+j:8*s+j+1]) for j in range(8)]
                for p in range(0,8,2):
                    for i in range(p+2,8):
                        Z[i]=Z[i]-(E[i,p]*Z[p]+E[i,p+1]*Z[p+1])
                for p in range(0,8,2):
                    Z[p+1]=Z[p+1]-E[p+1,p]*Z[p]
                Z=[z*r for z,r in zip(Z,ra)]
                def dot8(X):
                    m=[z*x for z,x in zip(Z,X)]
                    return ((m[0]+m[1])+(m[2]+m[3]))+((m[4]+m[5])+(m[6]+m[7]))
                rows.append(St-dot8(W)); trows.append(Tt-dot8(V))
            S=jnp.concatenate(rows,0); T=jnp.concatenate(trows,0)
    return jnp.concatenate(U,0), jnp.concatenate(M,0)

def chol_kernel(a_ref, l_ref, m_ref, w_ref, d_ref):
    def blk(i, j):
        return (pl.ds(128 * i, 128), pl.ds(128 * j, 128))

    zero = jnp.zeros((128, 128), jnp.float32)
    for i in range(6):
        for j in range(6):
            if j > i:
                l_ref[blk(i, j)] = zero
                m_ref[blk(i, j)] = zero
                continue
            v = a_ref[blk(i, j)]
            if i // 2 == j // 2:
                v = 0.5 * (v + (v.T if i == j else a_ref[blk(j, i)].T))
            w_ref[blk(i, j)] = v
    tri = lax.broadcasted_iota(jnp.int32, (128, 128), 0) >= lax.broadcasted_iota(jnp.int32, (128, 128), 1)

    def step(k, carry):
        at = pl.multiple_of(k * 128, 128)
        here = (pl.ds(at, 128), pl.ds(at, 128))
        U, M = base(w_ref[here])
        l_ref[here] = jnp.where(tri, U.T, 0.0)
        m_ref[here] = M
        d_ref[...] = M
        for kk in range(6):
            @pl.when(k == kk)
            def _(kk=kk):
                M = d_ref[...]
                if kk < 5:
                    n, r0 = 128 * (5 - kk), 128 * (kk + 1)
                    P = nt(w_ref[pl.ds(r0, n), pl.ds(128 * kk, 128)], M)
                    l_ref[pl.ds(r0, n), pl.ds(128 * kk, 128)] = P
                    for j in range(kk + 1, 6):
                        q0 = 128 * (j - kk - 1)
                        w_ref[pl.ds(128 * j, n - q0), pl.ds(128 * j, 128)] -= nt(P[q0:], P[q0:q0 + 128])
                if kk > 0:
                    acc = nn(l_ref[pl.ds(128 * kk, 128), pl.ds(0, 128 * kk)], m_ref[pl.ds(0, 128 * kk), pl.ds(0, 128 * kk)])
                    m_ref[pl.ds(128 * kk, 128), pl.ds(0, 128 * kk)] = -nn(M, acc)
        return carry

    lax.fori_loop(0, 6, step, 0)


def order_offsets():
    rest = [(n // 16, (n // 4) % 4, (n // 2) % 2, n % 2) for n in range(1, 32)]
    total = (16, 16, 16, 16)
    load = [0, 0, 0, 0]
    out = []

    def use(o):
        dz, dy, dx, dk = o
        return (dz, dx, int(dy in (1, 2)), int(dy in (2, 3)))

    while rest:
        share = (len(out) + 1) / 31
        best = min(rest, key=lambda o: (sum((a + b - t * share) ** 2 for a, b, t in zip(load, use(o), total)), (o[0] * 7 + o[1] * 3 + o[2] * 5 + o[3] * 11) % 13))
        rest.remove(best)
        out.append(best)
        load = [a + b for a, b in zip(load, use(best))]
    return out


OFFSETS = order_offsets()
BATCH = (8, 3, 3, 3)


def spread(w, g, s, col):
    if col == 0:
        return s(0)
    if col == 5:
        return s(3)
    if col == 1:
        return s(1) * w[g, 0:1]
    if col == 2:
        return s(1) * w[g, 1:2] + s(2) * w[g, 2:3]
    if col == 3:
        return s(1) * w[g, 3:4] + s(2) * w[g, 4:5]
    return s(2) * w[g, 5:6]


def front_kernel(rows_ref, cols_ref, child_hbm, base_hbm, res, child, packed, arr, base, lbuf, cbuf, w_in, wb, top, work, low, inv, diag, inv_hi, inv_lo,
                 lsem, ssem, rsem, dsem, wsem, csem, ysem, xsem, ksem):
    pair = lax.axis_index("pair")
    z = lax.axis_index("bit")
    f = lax.axis_index("front")
    y, x, k = f // 4, (f // 2) % 2, f % 2
    me = z * 16 + f

    def at(dz, dy, dx, dk):
        return (pair, (z + dz) % 2, ((y + dy) % 4) * 4 + ((x + dx) % 2) * 2 + (k + dk) % 2)

    child_copy = pltpu.make_async_copy(child_hbm, child, lsem.at[0])
    base_copy = pltpu.make_async_copy(base_hbm.at[0, 0], base, lsem.at[1])
    child_copy.start()
    base_copy.start()
    bar = pltpu.get_barrier_semaphore()
    for n in range(1, 32):
        pl.semaphore_signal(bar, inc=1, device_id=at(n // 16, (n // 4) % 4, (n // 2) % 2, n % 2), device_id_type=MESH)
    pl.semaphore_wait(bar, 31)

    c1, c2 = cols_ref[0, 1], cols_ref[0, 2]
    lines = [jnp.broadcast_to(jnp.where(c, 1.0, 0.0), (1, 128)) for c in (c1 == 1, c1 == 2, c2 == 2, c1 == 3, c2 == 3, c2 == 4)]
    masks = jnp.concatenate(lines + [jnp.zeros((2, 128), jnp.float32)], 0)
    w_in[...] = masks
    wb[z] = masks
    wcopy = pltpu.make_async_remote_copy(
        src_ref=w_in, dst_ref=wb.at[z], send_sem=wsem.at[0], recv_sem=wsem.at[1],
        device_id=at(1, 0, 0, 0), device_id_type=MESH)
    wcopy.start()
    child_copy.wait()

    def tile_for(d):
        target = 32 * (f % 8) + 2 * (d % 16) + d // 16
        i = jnp.int32(0)
        for t in range(14):
            i = jnp.where(rows_ref[t] == target, t + 1, i)
        return jnp.where(i > 0, child[jnp.maximum(i - 1, 0)], 0.0)

    source = (f == 0) | (f == 8)
    half = z * 2 + y // 2
    widths = (256, 384, 512)

    def child_send(b, q):
        n = widths[q]
        return pltpu.make_async_remote_copy(
            src_ref=lbuf.at[3 * b + q, :, pl.ds(0, n)], dst_ref=cbuf.at[half, :, pl.ds(0, n)], send_sem=dsem.at[b * 3 + q],
            recv_sem=csem.at[half], device_id=(pair, b, q), device_id_type=MESH)

    def own(b, q):
        return (f == q) & (z == b)

    @pl.when(source)
    def _():
        for q in (2, 1, 0):
            for b in range(2):
                lbuf[3 * b + q] = tile_for(16 * b + q)

                @pl.when(jnp.logical_not(own(b, q)))
                def _(b=b, q=q):
                    child_send(b, q).start()

    def offset(n):
        a, b = OFFSETS[n], OFFSETS[30 - n]
        return tuple(u + k * (v - u) for u, v in zip(a, b))

    def bulk(n):
        dz, dy, dx, dk = offset(n)
        to = at(dz, dy, dx, dk)
        return to, pltpu.make_async_remote_copy(
            src_ref=packed.at[n], dst_ref=arr.at[me], send_sem=ssem.at[n], recv_sem=rsem.at[me], device_id=to, device_id_type=MESH)

    def batch(lo, hi):
        for n in range(lo, hi):
            to, copy = bulk(n)
            packed[n] = tile_for(to[1] * 16 + to[2])
            copy.start()

    marks = [sum(BATCH[:i]) for i in range(5)]
    batch(0, marks[1])
    arr[me] = tile_for(me)
    base_copy.wait()
    wcopy.wait_recv()

    for q in range(3):
        n = widths[q]

        @pl.when(f == q)
        def _(q=q, n=n):
            for s in range(4):
                mine_too = (f == 0) & (half == s)

                @pl.when(jnp.logical_not(mine_too))
                def _(s=s):
                    pltpu.make_async_remote_copy(
                        src_ref=lbuf.at[0, :, pl.ds(0, n)], dst_ref=cbuf.at[s, :, pl.ds(0, n)], send_sem=dsem.at[0],
                        recv_sem=csem.at[s], device_id=at(1, 0, 0, 0), device_id_type=MESH).wait_recv()

                if q == 0:
                    @pl.when(mine_too)
                    def _(s=s):
                        cbuf[s, :, 0:256] = lbuf[3 * z, :, 0:256]
            row = pl.ds(pl.multiple_of((2 * q + z) * 128, 128), 128)
            for col in range(2 * q + 2):
                v = base[0, :, 128 * col:128 * col + 128]
                for g in range(2):
                    v = v + spread(wb, g, lambda c, g=g: cbuf[2 * g, :, 128 * c:128 * c + 128] + cbuf[2 * g + 1, :, 128 * c:128 * c + 128], col)
                top[row, 128 * col:128 * col + 128] = v

    def tile_copy(q, zz, send, recv, to):
        piece = top.at[pl.ds(pl.multiple_of((2 * q + zz) * 128, 128), 128), pl.ds(0, 256 * q + 256)]
        return pltpu.make_async_remote_copy(
            src_ref=piece, dst_ref=piece, send_sem=send, recv_sem=recv, device_id=to, device_id_type=MESH)

    mine = f % 4
    for q in range(3):
        @pl.when(f == q)
        def _(q=q):
            for n, dy in enumerate((2, 1, 3)):
                tile_copy(q, z, dsem.at[6 + n], ysem.at[0], at(0, dy, 0, 0)).start()
    batch(marks[1], marks[2])
    for q in range(3):
        @pl.when(mine == q)
        def _(q=q):
            @pl.when(y > 0)
            def _():
                tile_copy(q, z, dsem.at[6], ysem.at[0], at(0, 1, 0, 0)).wait_recv()

            for n, (dz, dx) in enumerate(((1, 1), (0, 1), (1, 0))):
                tile_copy(q, z, dsem.at[9 + n], xsem.at[2 * q + z], at(dz, 0, dx, 0)).start()
            tile_copy(q, z, dsem.at[(14 if q == 2 else 12) + z], ksem.at[2 * q + z], at(0, 0, 0, 1)).start()
    batch(marks[2], marks[3])
    for q in range(3):
        @pl.when(k == q % 2)
        def _(q=q):
            for zz in range(2):
                @pl.when((mine != q) | (z != zz))
                def _(zz=zz):
                    tile_copy(q, zz, dsem.at[9], xsem.at[2 * q + zz], at(0, 0, 1, 0)).wait_recv()
                    tile_copy(q, zz, dsem.at[(14 if q == 2 else 12) + zz], ksem.at[2 * q + zz], at(0, 0, 0, 1)).start()
    batch(marks[3], marks[4])
    for q in range(3):
        @pl.when(k != q % 2)
        def _(q=q):
            for zz in range(2):
                tile_copy(q, zz, dsem.at[9], ksem.at[2 * q + zz], at(0, 0, 0, 1)).wait_recv()
    batch(marks[4], 31)

    chol_kernel(top, low, inv, work, diag)
    v = inv[...]
    hi = v.astype(jnp.bfloat16)
    inv_hi[...] = hi
    inv_lo[...] = (v - hi.astype(jnp.float32)).astype(jnp.bfloat16)

    def slot_of(e):
        return ((y + e // 4) % 2) * 4 + ((x + e // 2) % 2) * 2 + (k + e) % 2

    for step in range(4):
        rows = []
        for e in (2 * step, 2 * step + 1):
            j = slot_of(e)
            for g in range(2):
                for h in range(2):
                    src = g * 16 + h * 8 + j

                    @pl.when(src != me)
                    def _(src=src):
                        pltpu.make_async_remote_copy(
                            src_ref=packed.at[0], dst_ref=arr.at[src], send_sem=ssem.at[0], recv_sem=rsem.at[src],
                            device_id=at(1, 0, 0, 0), device_id_type=MESH).wait_recv()
            cols = []
            for col in range(6):
                v = base[j, :, 128 * col:128 * col + 128]
                for g in range(2):
                    v = v + spread(wb, g, lambda c, g=g: arr[g * 16 + j, :, 128 * c:128 * c + 128] + arr[g * 16 + 8 + j, :, 128 * c:128 * c + 128], col)
                cols.append(v)
            rows.append(jnp.concatenate(cols, 1))
        a = jnp.concatenate(rows, 0)
        a_hi = a.astype(jnp.bfloat16)
        a_lo = (a - a_hi.astype(jnp.float32)).astype(jnp.bfloat16)
        for s in range(3):
            n = 256 * s + 256
            m_hi, m_lo = inv_hi[n - 256:n, :n], inv_lo[n - 256:n, :n]
            v = (nt(a_lo[:, :n], m_hi, None) + nt(a_hi[:, :n], m_lo, None)) + nt(a_hi[:, :n], m_hi, None)
            for e in (0, 1):
                res[0, 0, slot_of(2 * step + e), :, n - 256:n] = v[128 * e:128 * e + 128]
        for e in (2 * step, 2 * step + 1):
            @pl.when((slot_of(e) == 0) & (f <= 2))
            def _(e=e):
                res[0, 0, 0] = low[pl.ds(pl.multiple_of((2 * f + z) * 128, 128), 128), :]

    for n in range(31):
        bulk(n)[1].wait_send()
    wcopy.wait_send()

    @pl.when(source)
    def _():
        for q in range(3):
            for b in range(2):
                @pl.when(jnp.logical_not(own(b, q)))
                def _(b=b, q=q):
                    child_send(b, q).wait_send()

    for q in range(3):
        @pl.when(f == q)
        def _(q=q):
            for n in range(3):
                tile_copy(q, z, dsem.at[6 + n], ysem.at[0], at(0, 1, 0, 0)).wait_send()

        @pl.when(mine == q)
        def _(q=q):
            for n in range(3):
                tile_copy(q, z, dsem.at[9 + n], xsem.at[2 * q + z], at(0, 0, 1, 0)).wait_send()

        @pl.when(k == q % 2)
        def _(q=q):
            for zz in range(2):
                tile_copy(q, zz, dsem.at[(14 if q == 2 else 12) + zz], ksem.at[2 * q + zz], at(0, 0, 0, 1)).wait_send()


def fronts(rows, cols, tiles, base_tiles):
    f32 = jnp.float32
    square = pltpu.VMEM((768, 768), f32)
    dma = pltpu.SemaphoreType.DMA
    return pl.pallas_call(
        front_kernel,
        out_shape=jax.ShapeDtypeStruct((1, 1, 8, 128, 768), f32),
        in_specs=[SM, SM, ANY, ANY],
        out_specs=VM,
        scratch_shapes=[
            pltpu.VMEM((14, 128, 512), f32),
            pltpu.VMEM((31, 128, 512), f32),
            pltpu.VMEM((32, 128, 512), f32),
            pltpu.VMEM((8, 128, 768), f32),
            pltpu.VMEM((6, 128, 512), f32),
            pltpu.VMEM((4, 128, 512), f32),
            pltpu.VMEM((8, 128), f32),
            pltpu.VMEM((2, 8, 128), f32),
            square, square, square, square,
            pltpu.VMEM((128, 128), f32),
            pltpu.VMEM((768, 768), jnp.bfloat16),
            pltpu.VMEM((768, 768), jnp.bfloat16),
            dma((2,)), dma((31,)), dma((32,)), dma((16,)), dma((2,)), dma((4,)), dma((1,)), dma((6,)), dma((6,)),
        ],
        compiler_params=pltpu.CompilerParams(collective_id=0, has_side_effects=True, vmem_limit_bytes=46 << 20),
        name="fronts",
    )(rows, cols, tiles, base_tiles)


def body(child_block, child_rows, child_cols, parent_base):
    return fronts(child_rows[0, 0], child_cols, child_block[0, 0], parent_base)


def solution(mesh):
    mesh = Mesh(mesh.devices.reshape(4, 2, 16), ("pair", "bit", "front"))
    cube = ("pair", "bit")
    placed = (P(cube, "front"), P(cube, "front"), P(cube), P(cube, "front"))
    return jax.shard_map(body, mesh=mesh, in_specs=placed, out_specs=P(cube, "front"), check_vma=False)
```

profile of v0, /device:TPU:31, one launch (start us, length us, event | category | flops | bytes accessed | tf_op | source)
XLA Modules:
  0.0 137.5 jit_solution(17608036791737283074)
XLA Ops:
  0.0 0.0 copy-start
  0.0 1.9 %copy-done = f32[1,1,8,128,768]{4,3,2,1,0:T(8,128)S(1)} copy-done((f32[1,1,8,128,768]{4,3,2,1,0:T(8,128)S(1)}, f32[1,1,8,128,768]{4,3,2,1,0:T(8,128)}, u32[]{:S(2)}) %copy-start) | copy-done | bytes 3145752
  1.9 0.0 copy-start.1
  1.9 0.7 copy-done.1
  2.5 0.0 copy-start.2
  2.5 0.7 copy-done.2
  3.2 132.7 %fronts.1 = f32[1,1,8,128,768]{4,3,2,1,0:T(8,128)S(1)} custom-call(s32[14]{0:T(128)S(1)} %bitcast.2, s32[1,4]{1,0:T(1,128)S(1)} %copy-done.2, f32[14,128,512]{2,1,0:T(8,128)} %bitcast.3, f32[1,1,8,128,768]{4,3,2,1,0:T(8,128)S(1)} %copy-done), custom_call_target="tpu_custom_call" | custom-call | tf_op jit(solution)/shard_map/fronts/pallas_call | solution.py:377
  135.9 1.7 %copy.6 = f32[1,1,8,128,768]{4,3,2,1,0:T(8,128)} copy(f32[1,1,8,128,768]{4,3,2,1,0:T(8,128)S(1)} %fronts.1) | data formatting | bytes 6291456
Async XLA Ops:
  0.0 1.9 %copy-start = (f32[1,1,8,128,768]{4,3,2,1,0:T(8,128)S(1)}, f32[1,1,8,128,768]{4,3,2,1,0:T(8,128)}, u32[]{:S(2)}) copy-start(f32[1,1,8,128,768]{4,3,2,1,0:T(8,128)} %base_hbm.1) | copy-start | bytes 9437188
  1.9 0.7 copy-start.1
  2.5 0.7 copy-start.2
where the time goes:
time: 138 us
  Pallas kernels  133 us (96%)
  local copies, waits for them, and re-layouts  4.87 us (4%)
    pallas_call x1, Pallas kernels, fronts(): pl.pallas_call(front_kernel, out_shape=jax.ShapeDtypeStruct((1, 1, 8, 128...  133 us
    unnamed x7, local copies, waits for them, and re-layouts  4.87 us

commit v1 on v0

--- a/solution.py
+++ b/solution.py
@@ -114,26 +114,34 @@
     lax.fori_loop(0, 6, step, 0)
 
 
+STEPS = (((0, 0, 0), (1, 1, 0)), ((0, 0, 1), (1, 1, 1)), ((0, 1, 0), (1, 0, 0)), ((0, 1, 1), (1, 0, 1)))
+
+
 def order_offsets():
-    rest = [(n // 16, (n // 4) % 4, (n // 2) % 2, n % 2) for n in range(1, 32)]
-    total = (16, 16, 16, 16)
-    load = [0, 0, 0, 0]
-    out = []
-
     def use(o):
         dz, dy, dx, dk = o
         return (dz, dx, int(dy in (1, 2)), int(dy in (2, 3)))
 
-    while rest:
-        share = (len(out) + 1) / 31
-        best = min(rest, key=lambda o: (sum((a + b - t * share) ** 2 for a, b, t in zip(load, use(o), total)), (o[0] * 7 + o[1] * 3 + o[2] * 5 + o[3] * 11) % 13))
-        rest.remove(best)
-        out.append(best)
-        load = [a + b for a, b in zip(load, use(best))]
-    return out
-
-
-OFFSETS = order_offsets()
+    def even(rest):
+        out, load, count = [], [0, 0, 0, 0], len(rest)
+        total = [sum(c) for c in zip(*map(use, rest))]
+        while rest:
+            share = (len(out) + 1) / count
+            best = min(rest, key=lambda o: (sum((a + b - t * share) ** 2 for a, b, t in zip(load, use(o), total)), rank[o]))
+            rest.remove(best)
+            out.append(best)
+            load = [a + b for a, b in zip(load, use(best))]
+        return out
+
+    every = [(n // 16, (n // 4) % 4, (n // 2) % 2, n % 2) for n in range(1, 32)]
+    rank = {o: (o[0] * RANK[0] + o[1] * RANK[1] + o[2] * RANK[2] + o[3] * RANK[3]) % 31 for o in every}
+    final = [o for o in every if (o[1] % 2, o[2], o[3]) in STEPS[3]]
+    return even([o for o in every if o not in final]), even(list(final))
+
+
+RANK = (3, 17, 5, 2)
+EARLY, LATE = order_offsets()
+OFFSETS = (EARLY + LATE, EARLY[::-1] + LATE[::-1])
 BATCH = (8, 3, 3, 3)
 
 
@@ -213,7 +221,7 @@
                     child_send(b, q).start()
 
     def offset(n):
-        a, b = OFFSETS[n], OFFSETS[30 - n]
+        a, b = OFFSETS[0][n], OFFSETS[1][n]
         return tuple(u + k * (v - u) for u, v in zip(a, b))
 
     def bulk(n):
@@ -305,7 +313,8 @@
     inv_lo[...] = (v - hi.astype(jnp.float32)).astype(jnp.bfloat16)
 
     def slot_of(e):
-        return ((y + e // 4) % 2) * 4 + ((x + e // 2) % 2) * 2 + (k + e) % 2
+        ey, ex, ek = STEPS[e // 2][e % 2]
+        return ((y + ey) % 2) * 4 + ((x + ex) % 2) * 2 + (k + ek) % 2
 
     for step in range(4):
         rows = []

time: 138 us -> 129 us (0.935); the launches traced: 138 us -> 127 us
  Pallas kernels: 133 us -> 122 us
    pallas_call x1, Pallas kernels: 133 us -> 122 us  [fronts(): pl.pallas_call(front_kernel, out_shape=jax.ShapeDtypeStruct((1, 1, 8, 128...]
where the time goes in v1:
time: 129 us; the launch traced here: 127 us
  Pallas kernels  122 us (95%)
  local copies, waits for them, and re-layouts  4.87 us (4%)
    pallas_call x1, Pallas kernels, fronts(): pl.pallas_call(front_kernel, out_shape=jax.ShapeDtypeStruct((1, 1, 8, 128...  122 us
    unnamed x7, local copies, waits for them, and re-layouts  4.87 us

profile of v1, /device:TPU:31, one launch (start us, length us, event | category | flops | bytes accessed | tf_op | source)
XLA Modules:
  0.0 126.9 jit_solution(16161072949620334351)
XLA Ops:
  0.0 0.0 copy-start
  0.0 1.9 %copy-done = f32[1,1,8,128,768]{4,3,2,1,0:T(8,128)S(1)} copy-done((f32[1,1,8,128,768]{4,3,2,1,0:T(8,128)S(1)}, f32[1,1,8,128,768]{4,3,2,1,0:T(8,128)}, u32[]{:S(2)}) %copy-start) | copy-done | bytes 3145752
  1.9 0.0 copy-start.1
  1.9 0.7 copy-done.1
  2.5 0.0 copy-start.2
  2.5 0.7 copy-done.2
  3.2 122.0 %fronts.1 = f32[1,1,8,128,768]{4,3,2,1,0:T(8,128)S(1)} custom-call(s32[14]{0:T(128)S(1)} %bitcast.2, s32[1,4]{1,0:T(1,128)S(1)} %copy-done.2, f32[14,128,512]{2,1,0:T(8,128)} %bitcast.3, f32[1,1,8,128,768]{4,3,2,1,0:T(8,128)S(1)} %copy-done), custom_call_target="tpu_custom_call" | custom-call | tf_op jit(solution)/shard_map/fronts/pallas_call | solution.py:386
  125.2 1.7 %copy.6 = f32[1,1,8,128,768]{4,3,2,1,0:T(8,128)} copy(f32[1,1,8,128,768]{4,3,2,1,0:T(8,128)S(1)} %fronts.1) | data formatting | bytes 6291456
Async XLA Ops:
  0.0 1.9 %copy-start = (f32[1,1,8,128,768]{4,3,2,1,0:T(8,128)S(1)}, f32[1,1,8,128,768]{4,3,2,1,0:T(8,128)}, u32[]{:S(2)}) copy-start(f32[1,1,8,128,768]{4,3,2,1,0:T(8,128)} %base_hbm.1) | copy-start | bytes 9437188
  1.9 0.7 copy-start.1
  2.5 0.7 copy-start.2
